TPU v7x, 768 devices: a whole 4x8x12 slice. The times are simulated.
768 devices in a mesh: gx: 12 (over z), gy: 4 (over x), gz: 16 (over y, core).
Axes of the slice: x: 4, y: 8, z: 12, core: 2. Of those that a mesh axis runs over, the one named last changes fastest.
Arguments:
- markers: float32 [4, 96, 256, 2048], P(None, 'gx', 'gy', 'gz'), may hold values from 0 to 1
- velocity: float32 [96, 256, 2048], P('gx', 'gy', 'gz'), may hold values from -0.45 to 0.45
- patch_boxes: int32 [4, 49152], P(None, ('gx', 'gy', 'gz')), may hold values from 0 to 96, as said below
- send_pick: int32 [12, 4, 16, 64, 2], P('gx', 'gy', 'gz'), may hold values from 0 to 63
- recv_pick: int32 [12, 4, 16, 64, 2], P('gx', 'gy', 'gz'), may hold values from 0 to 63
- pair_count: int32 [12, 4, 16, 64], P('gx', 'gy', 'gz'), may hold values from 0 to 2, as said below
Outputs:
- advected: float32 [4, 96, 256, 2048], P(None, 'gx', 'gy', 'gz')
- bubble_force: float32 [49152, 4096], P(('gx', 'gy', 'gz'))
Inputs may be any that keep to these rules, and one draw needn't show every extreme that they name: `patch_boxes`: patch boxes lie inside their owner's block: first cells along x, y, z run to at most 4, 32, 96; the marker function is below 4. `pair_count`: A device's count to itself is 0; in every slab the first device has 2 pairs to every other peer.
All inputs are finite; a program needn't handle non-finite values.
Results may differ from a plain program's by a relative error of at most 0.005.
Values may be sent and summed in bfloat16 or wider, within the bound.
A program may use at most 32 MiB of HBM per device.

v0:
```python
import jax
import jax.numpy as jnp
from jax import lax
from jax.sharding import PartitionSpec as P

BAND = 4
PATCH = 32
FLAT = 4096


def extended(x, sides, width):
    for axis, dim in sides:
        count, length = (lax.axis_size(axis), x.shape[dim])
        up = [(i, (i + 1) % count) for i in range(count - 1)]
        down = [(j, i) for i, j in up]
        last = lax.slice_in_dim(x, length - width, length, axis=dim)
        initial = lax.slice_in_dim(x, 0, width, axis=dim)
        before = lax.ppermute(last, axis, up)
        after = lax.ppermute(initial, axis, down)
        x = jnp.concatenate([before, x, after], axis=dim)
    return x


def advect_sweep(padded_markers, padded_velocity, markers):
    face = 0.5 * (padded_velocity[:-1] + padded_velocity[1:])
    flux = face[None] * jnp.where(face[None] > 0, padded_markers[:, :-1], padded_markers[:, 1:])
    return markers - (flux[:, 1:] - flux[:, :-1]) + markers * (face[1:] - face[:-1])[None]


def cut_table(markers, boxes):
    mark_count, depth, width_y, width_z = markers.shape
    bubble_count = boxes.shape[1]
    high = lax.Precision.HIGHEST
    first_row = boxes[0] * depth + boxes[1]
    wanted = first_row[:, None] + jnp.arange(BAND, dtype=jnp.int32)[None, :]
    plane_sel = (
        wanted.reshape(-1)[:, None] == jnp.arange(mark_count * depth, dtype=jnp.int32)[None, :]
    ).astype(jnp.float32)
    planes = jnp.dot(
        plane_sel,
        markers.reshape(mark_count * depth, width_y * width_z),
        precision=high,
        preferred_element_type=jnp.float32,
    )
    planes = planes.reshape(bubble_count, BAND, width_y, width_z)
    offsets = jnp.arange(PATCH, dtype=jnp.int32)[None, :, None]
    y_sel = (
        boxes[2][:, None, None] + offsets == jnp.arange(width_y, dtype=jnp.int32)[None, None, :]
    ).astype(jnp.float32)
    z_sel = (
        boxes[3][:, None, None] + offsets == jnp.arange(width_z, dtype=jnp.int32)[None, None, :]
    ).astype(jnp.float32)
    window = jnp.einsum(
        "bkyz,bpy->bkpz", planes, y_sel, precision=high, preferred_element_type=jnp.float32
    )
    window = jnp.einsum(
        "bkpz,bqz->bkpq", window, z_sel, precision=high, preferred_element_type=jnp.float32
    )
    return window.reshape(bubble_count, FLAT).astype(jnp.bfloat16)


def on_device(markers, velocity, patch_boxes, send_pick, recv_pick, pair_count):
    mark_count = markers.shape[0]
    stacked = jnp.concatenate([markers, velocity[None]], axis=0)
    padded = extended(stacked.astype(jnp.bfloat16), (("gx", 1),), 1).astype(stacked.dtype)
    advected = advect_sweep(padded[:mark_count], padded[mark_count], markers)
    gy_size = lax.axis_size("gy")
    gz_size = lax.axis_size("gz")
    peer_count = gy_size * gz_size
    bubble_count = patch_boxes.shape[1]
    slot_count = send_pick.shape[-1]
    send_rows = send_pick.reshape(peer_count * slot_count)
    recv_rows = recv_pick.reshape(peer_count * slot_count)
    counts = pair_count.reshape(peer_count)
    used_slot = (jnp.arange(slot_count, dtype=jnp.int32)[None, :] < counts[:, None]).reshape(-1, 1)
    patch_table = cut_table(markers, patch_boxes)
    bubble_ids = jnp.arange(bubble_count, dtype=jnp.int32)[None, :]
    pick_near = (recv_rows[:, None] == bubble_ids).astype(jnp.bfloat16)
    pick_far = (send_rows[:, None] == bubble_ids).astype(jnp.bfloat16)
    picked = jnp.dot(pick_far, patch_table, preferred_element_type=jnp.float32).astype(jnp.bfloat16)
    home_patch = jnp.dot(pick_near, patch_table, preferred_element_type=jnp.float32).astype(
        jnp.bfloat16
    )
    outgoing = jnp.where(used_slot, picked, jnp.zeros_like(picked))
    home_wide = home_patch.astype(jnp.float32)
    incoming = lax.all_to_all(
        outgoing.reshape(peer_count, slot_count, FLAT),
        ("gy", "gz"),
        split_axis=0,
        concat_axis=0,
        tiled=True,
    )
    incoming = incoming.reshape(peer_count * slot_count, FLAT)
    far_wide = incoming.astype(jnp.float32)
    film = 0.8 * home_wide * far_wide
    near_force = (film * (1.0 - home_wide)).astype(jnp.bfloat16)
    far_force = (film * (1.0 - far_wide)).astype(jnp.bfloat16)
    returned = lax.all_to_all(
        far_force.reshape(peer_count, slot_count, FLAT),
        ("gy", "gz"),
        split_axis=0,
        concat_axis=0,
        tiled=True,
    )
    returned = returned.reshape(peer_count * slot_count, FLAT)
    contract = (((0,), (0,)), ((), ()))
    totals = lax.dot_general(pick_near, near_force, contract, preferred_element_type=jnp.float32)
    totals = totals + lax.dot_general(
        pick_far, returned, contract, preferred_element_type=jnp.float32
    )
    return (advected, totals)


def solution(mesh):
    placed = (
        P(None, "gx", "gy", "gz"),
        P("gx", "gy", "gz"),
        P(None, ("gx", "gy", "gz")),
        P("gx", "gy", "gz", None, None),
        P("gx", "gy", "gz", None, None),
        P("gx", "gy", "gz", None),
    )
    return jax.shard_map(
        on_device,
        mesh=mesh,
        in_specs=placed,
        out_specs=(P(None, "gx", "gy", "gz"), P(("gx", "gy", "gz"), None)),
        check_vma=False,
    )
```

profile of v0, /device:TPU:1, one launch (start us, length us, event | category | flops | bytes accessed | tf_op | source)
XLA Modules:
  0.0 113.0 jit_solution(17105098446717666069)
XLA Ops:
  0.6 0.8 slice_bitcast_fusion
  1.5 1.8 %copy.25 = f32[4,8,64,128]{3,1,2,0:T(8,128)S(1)} copy(f32[4,8,64,128]{3,2,1,0:T(8,128)} %param.6) | data formatting | bytes 2097152
  3.3 0.2 copy.19
  3.6 3.5 %fusion.13 = f32[64,4,64,128]{3,0,2,1:T(8,128)S(1)} fusion(f32[64,128,32,1]{1,0,2,3:T(8,128)S(1)} %bitcast.59, s32[64,4]{0,1:T(4,128)S(1)} %iota_add_fusion.2), kind=kOutput, calls=%fused_computation.20 | convolution fusion | flops 805314560 | bytes 9438208 | tf_op jit(solution)/shard_map/dot_general | solution.py:39
  7.1 10.7 %fusion = f32[64,32,4,128]{3,1,2,0:T(8,128)S(1)} fusion(f32[64,4,64,128]{3,0,2,1:T(8,128)S(1)} %fusion.13, s32[64,32]{1,0:T(8,128)S(1)} %get-tuple-element.12), kind=kOutput, calls=%fused_computation | convolution fusion | flops 805437440 | bytes 12591104 | tf_op jit(solution)/shard_map/bkyz,bpy->bkpz/dot_general | solution.py:53
  17.8 2.4 %fusion.6 = bf16[64,4,32,32]{3,2,1,0:T(8,128)(2,1)S(1)} fusion(f32[64,32,4,128]{3,1,2,0:T(8,128)S(1)} %fusion, s32[64,32]{1,0:T(8,128)S(1)} %get-tuple-element.11), kind=kOutput, calls=%fused_computation.12 | convolution fusion | flops 403177472 | bytes 4726784 | tf_op jit(solution)/shard_map/bkpz,bqz->bkpq/dot_general | solution.py:56
  20.2 2.2 %copy.11 = bf16[64,4,32,32]{0,3,2,1:T(8,128)(2,1)S(1)} copy(bf16[64,4,32,32]{3,2,1,0:T(8,128)(2,1)S(1)} %fusion.6) | data formatting | bytes 1048576 | tf_op jit(solution)/shard_map/convert_element_type | solution.py:59
  22.5 0.1 copy.12
  22.6 0.1 eq.99
  22.8 0.2 lt.26
  22.9 0.5 fusion.3
  23.5 1.5 %reshape.155 = bf16[64,2,4096]{2,1,0:T(2,128)(2,1)} reshape(bf16[128,4096]{1,0:T(8,128)(2,1)S(1)} %fusion.3) | data formatting | bytes 2097152 | tf_op jit(solution)/shard_map/reshape | solution.py:87
  24.9 15.4 %all-to-all-start = ((bf16[64,2,4096]{2,1,0:T(2,128)(2,1)}), bf16[64,2,4096]{2,1,0:T(2,128)(2,1)}, u32[]{:S(2)}, u32[]{:S(2)}) async-start(bf16[64,2,4096]{2,1,0:T(2,128)(2,1)} %reshape.155), calls=%async_computation | async-start | bytes 2097152 | tf_op jit(solution)/shard_map/all_to_all | solution.py:86
  40.4 0.1 copy.10
  40.5 0.1 eq.85
  40.6 28.2 %all-to-all-done = bf16[64,2,4096]{2,1,0:T(2,128)(2,1)} async-done(((bf16[64,2,4096]{2,1,0:T(2,128)(2,1)}), bf16[64,2,4096]{2,1,0:T(2,128)(2,1)}, u32[]{:S(2)}, u32[]{:S(2)}) %all-to-all-start) | async-done | bytes 1048608 | tf_op jit(solution)/shard_map/all_to_all | solution.py:86
  68.8 1.4 %reshape.158 = f32[128,4096]{1,0:T(8,128)S(1)} reshape(bf16[64,2,4096]{2,1,0:T(2,128)(2,1)} %all-to-all-done) | data formatting | bytes 3145728 | tf_op jit(solution)/shard_map/convert_element_type | solution.py:94
  70.2 2.3 %multiply_convert_fusion = (bf16[128,4096]{1,0:T(8,128)(2,1)}, f32[128,4096]{1,0:T(8,128)}) fusion(f32[128,4096]{1,0:T(8,128)S(1)} %reshape.158, bf16[64,4096]{0,1:T(8,128)(2,1)S(1)} %bitcast.57, s32[128]{0:T(128)S(1)} %eq.85), kind=kOutput, calls=%fused_computation.9 | convolution fusion | flops 70787072 | bytes 5767680 | tf_op jit(solution)/shard_map/dot_general | solution.py:81
  72.5 2.6 %reshape.156 = bf16[64,2,4096]{2,1,0:T(2,128)(2,1)} reshape(bf16[128,4096]{1,0:T(8,128)(2,1)} %get-tuple-element.9) | data formatting | bytes 2097152 | tf_op jit(solution)/shard_map/reshape | solution.py:99
  75.1 6.6 %all-to-all-start.1 = ((bf16[64,2,4096]{2,1,0:T(2,128)(2,1)}), bf16[64,2,4096]{2,1,0:T(2,128)(2,1)}, u32[]{:S(2)}, u32[]{:S(2)}) async-start(bf16[64,2,4096]{2,1,0:T(2,128)(2,1)} %reshape.156), calls=%async_computation.1 | async-start | bytes 2097152 | tf_op jit(solution)/shard_map/all_to_all | solution.py:98
  81.9 1.3 %collective-permute-start = (bf16[5,1,64,128]{3,2,1,0:T(8,128)(2,1)S(1)}, bf16[5,1,64,128]{3,2,1,0:T(8,128)(2,1)S(1)}, u32[]{:S(2)}, u32[]{:S(2)}) collective-permute-start(bf16[5,1,64,128]{3,2,1,0:T(8,128)(2,1)S(1)} %get-tuple-element.4), channel_id=1, source_target_pairs={{0,64},{64,128},{128,192},{192,256},{256,320},{320,384},{384,448},... | collective-permute-start | bytes 245768 | tf_op jit(solution)/shard_map/ppermute | solution.py:18
  83.2 1.3 %collective-permute-start.1 = (bf16[5,1,64,128]{3,2,1,0:T(8,128)(2,1)S(1)}, bf16[5,1,64,128]{3,2,1,0:T(8,128)(2,1)S(1)}, u32[]{:S(2)}, u32[]{:S(2)}) collective-permute-start(bf16[5,1,64,128]{3,2,1,0:T(8,128)(2,1)S(1)} %get-tuple-element.5), channel_id=1, source_target_pairs={{64,0},{128,64},{192,128},{256,192},{320,256},{384,320},{448,384},... | collective-permute-start | bytes 245768 | tf_op jit(solution)/shard_map/ppermute | solution.py:19
  84.5 0.2 collective-permute-done
  84.6 4.1 %collective-permute-done.1 = bf16[5,1,64,128]{3,2,1,0:T(8,128)(2,1)S(1)} collective-permute-done((bf16[5,1,64,128]{3,2,1,0:T(8,128)(2,1)S(1)}, bf16[5,1,64,128]{3,2,1,0:T(8,128)(2,1)S(1)}, u32[]{:S(2)}, u32[]{:S(2)}) %collective-permute-start.1) | collective-permute-done | bytes 81952 | tf_op jit(solution)/shard_map/ppermute | solution.py:19
  88.9 0.2 maximum_convert_fusion
  89.0 0.2 fusion.9
  89.3 1.2 %fusion.12 = f32[4,8,64,128]{3,2,1,0:T(8,128)} fusion(f32[4,8,64,128]{3,2,1,0:T(8,128)S(1)} %copy-done, f32[4,9,64,128]{3,2,1,0:T(8,128)S(1)} %fusion.9, f32[8,64,128]{2,1,0:T(8,128)S(1)} %fusion.24), kind=kLoop, calls=%fused_computation.19 | loop fusion | flops 1048576 | bytes 4456448 | tf_op jit(solution)/shard_map/add | solution.py:27
  90.5 0.7 copy-done.1
  91.2 0.6 fusion.10
  91.8 18.4 %all-to-all-done.1 = bf16[64,2,4096]{2,1,0:T(2,128)(2,1)} async-done(((bf16[64,2,4096]{2,1,0:T(2,128)(2,1)}), bf16[64,2,4096]{2,1,0:T(2,128)(2,1)}, u32[]{:S(2)}, u32[]{:S(2)}) %all-to-all-start.1) | async-done | bytes 1048608 | tf_op jit(solution)/shard_map/all_to_all | solution.py:98
  110.2 1.5 %reshape.157 = bf16[128,4096]{1,0:T(8,128)(2,1)S(1)} reshape(bf16[64,2,4096]{2,1,0:T(2,128)(2,1)} %all-to-all-done.1) | data formatting | bytes 2097152 | tf_op jit(solution)/shard_map/reshape | solution.py:105
  111.7 1.4 %convolution_add_fusion = f32[64,4096]{1,0:T(8,128)} fusion(f32[64,4096]{1,0:T(8,128)S(1)} %fusion.10, bf16[128,4096]{1,0:T(8,128)(2,1)S(1)} %reshape.157, s32[128]{0:T(128)S(1)} %eq.99), kind=kOutput, calls=%fused_computation.5 | convolution fusion | flops 67379200 | bytes 3146240 | tf_op jit(solution)/shard_map/dot_general | solution.py:108
  (19 shorter events, 0.4 us)
Async XLA Ops:
  20.2 2.3 %copy-start.3 = (s32[1,1,1,64,2]{3,4,2,1,0:T(2,128)S(1)}, s32[1,1,1,64,2]{3,4,2,1,0:T(2,128)}, u32[]{:S(2)}) copy-start(s32[1,1,1,64,2]{3,4,2,1,0:T(2,128)} %param.9) | copy-start | bytes 1540
  20.2 2.5 %copy-start.5 = (s32[1,1,1,64]{3,2,1,0:T(1,128)S(1)}, s32[1,1,1,64]{3,2,1,0:T(1,128)}, u32[]{:S(2)}) copy-start(s32[1,1,1,64]{3,2,1,0:T(1,128)} %param.11) | copy-start | bytes 772
  23.4 16.9 %copy-start.4 = (s32[1,1,1,64,2]{3,4,2,1,0:T(2,128)S(1)}, s32[1,1,1,64,2]{3,4,2,1,0:T(2,128)}, u32[]{:S(2)}) copy-start(s32[1,1,1,64,2]{3,4,2,1,0:T(2,128)} %param.10) | copy-start | bytes 1540
  24.9 43.9 %all-to-all-start = ((bf16[64,2,4096]{2,1,0:T(2,128)(2,1)}), bf16[64,2,4096]{2,1,0:T(2,128)(2,1)}, u32[]{:S(2)}, u32[]{:S(2)}) async-start(bf16[64,2,4096]{2,1,0:T(2,128)(2,1)} %reshape.155), calls=%async_computation | async-start | bytes 2097152 | tf_op jit(solution)/shard_map/all_to_all | solution.py:86
  72.5 9.2 %copy-start = (f32[4,8,64,128]{3,2,1,0:T(8,128)S(1)}, f32[4,8,64,128]{3,2,1,0:T(8,128)}, u32[]{:S(2)}) copy-start(f32[4,8,64,128]{3,2,1,0:T(8,128)} %param.6) | copy-start | bytes 3145732
  75.1 6.7 %copy-start.2 = (f32[8,64,128]{2,1,0:T(8,128)S(1)}, f32[8,64,128]{2,1,0:T(8,128)}, u32[]{:S(2)}) copy-start(f32[8,64,128]{2,1,0:T(8,128)} %param.7) | copy-start | bytes 786436
  75.1 35.1 %all-to-all-start.1 = ((bf16[64,2,4096]{2,1,0:T(2,128)(2,1)}), bf16[64,2,4096]{2,1,0:T(2,128)(2,1)}, u32[]{:S(2)}, u32[]{:S(2)}) async-start(bf16[64,2,4096]{2,1,0:T(2,128)(2,1)} %reshape.156), calls=%async_computation.1 | async-start | bytes 2097152 | tf_op jit(solution)/shard_map/all_to_all | solution.py:98
  81.9 2.8 %collective-permute-start = (bf16[5,1,64,128]{3,2,1,0:T(8,128)(2,1)S(1)}, bf16[5,1,64,128]{3,2,1,0:T(8,128)(2,1)S(1)}, u32[]{:S(2)}, u32[]{:S(2)}) collective-permute-start(bf16[5,1,64,128]{3,2,1,0:T(8,128)(2,1)S(1)} %get-tuple-element.4), channel_id=1, source_target_pairs={{0,64},{64,128},{128,192},{192,256},{256,320},{320,384},{384,448},... | collective-permute-start | bytes 245768 | tf_op jit(solution)/shard_map/ppermute | solution.py:18
  83.2 5.6 %collective-permute-start.1 = (bf16[5,1,64,128]{3,2,1,0:T(8,128)(2,1)S(1)}, bf16[5,1,64,128]{3,2,1,0:T(8,128)(2,1)S(1)}, u32[]{:S(2)}, u32[]{:S(2)}) collective-permute-start(bf16[5,1,64,128]{3,2,1,0:T(8,128)(2,1)S(1)} %get-tuple-element.5), channel_id=1, source_target_pairs={{64,0},{128,64},{192,128},{256,192},{320,256},{384,320},{448,384},... | collective-permute-start | bytes 245768 | tf_op jit(solution)/shard_map/ppermute | solution.py:19
  89.3 2.0 %copy-start.1 = (f32[128,4096]{1,0:T(8,128)S(1)}, f32[128,4096]{1,0:T(8,128)}, u32[]{:S(2)}) copy-start(f32[128,4096]{1,0:T(8,128)} %get-tuple-element.10) | copy-start | bytes 6291460
where the time goes:
time: 114 us; the launch traced here: 113 us
  waiting for transfers between devices  50.9 us (45%)
  starting transfers between devices  24.6 us (22%)
  matrix products  21.3 us (19%)
  local copies, waits for them, and re-layouts  12.6 us (11%)
  other arithmetic  2.83 us (2%)
    all_to_all x1, waiting for transfers between devices, on_device(): lax.all_to_all(outgoing.reshape(peer_count, slot_count, FLAT), ('gy', 'gz...  28.2 us
    all_to_all x1, waiting for transfers between devices, on_device(): lax.all_to_all(far_force.reshape(peer_count, slot_count, FLAT), ('gy', 'g...  18.4 us
    all_to_all x1, starting transfers between devices, on_device(): lax.all_to_all(outgoing.reshape(peer_count, slot_count, FLAT), ('gy', 'gz...  15.4 us
    dot_general x1, matrix products, cut_table(): jnp.einsum('bkyz,bpy->bkpz', planes, y_sel, precision=high, preferred_ele...  10.7 us
    all_to_all x1, starting transfers between devices, on_device(): lax.all_to_all(far_force.reshape(peer_count, slot_count, FLAT), ('gy', 'g...  6.6 us
    ppermute x1, waiting for transfers between devices, extended(): after = lax.ppermute(initial, axis, down)  4.12 us
    dot_general x1, matrix products, cut_table(): jnp.dot(plane_sel, markers.reshape(mark_count * depth, width_y * width_z)...  3.52 us
    unnamed x16, local copies, waits for them, and re-layouts  2.98 us
  transfers between devices with their start and end apart: 4, of which 4 were waited for; matrix products, arithmetic and copies ran while one was open for 2% of the time, Pallas kernels for 0%

commit v1 on v0

v1 whole, which is shorter than its diff:
```python
import jax
import jax.numpy as jnp
from jax import lax
from jax.experimental import pallas as pl
from jax.experimental.pallas import tpu as pltpu
from jax.sharding import PartitionSpec as P

MESH = pl.DeviceIdType.MESH
BAND = 4
PATCH = 32
BUB = 64
NY = 8
NX = 4
NZ = 12
CHIPS = NX * NY
LANES = 128
UNUSED = 512.0
F32 = jnp.float32
BF16 = jnp.bfloat16


def cut_kernel(boxes, rows, out, tmp):
    lane = lax.broadcasted_iota(jnp.int32, (8, LANES), 1) // PATCH

    def one(b, _):
        base = (boxes[0, b] * 8 + boxes[1, b]) * 64 + boxes[2, b]
        z0 = boxes[3, b]
        for dx in range(BAND):
            cells = jnp.zeros((8, LANES), F32)
            for j in range(4):
                piece = rows[pl.ds(base + dx * 64 + j, 8, stride=4), :]
                piece = pltpu.roll(piece, lax.rem(PATCH * j - z0 + LANES, LANES), 1)
                cells = jnp.where(lane == j, piece, cells)
            tmp[pl.ds(pl.multiple_of(b * CHIPS + dx * 8, 8), 8), :] = cells
        return 0

    lax.fori_loop(0, BUB, one, 0)

    def put(s, _):
        out[s] = tmp[pl.ds(s, BUB, stride=CHIPS), :].astype(BF16)
        return 0

    lax.fori_loop(0, CHIPS, put, 0)


def cut(boxes, markers):
    return pl.pallas_call(
        cut_kernel,
        out_shape=jax.ShapeDtypeStruct((CHIPS, BUB, LANES), BF16),
        in_specs=[
            pl.BlockSpec(memory_space=pltpu.SMEM),
            pl.BlockSpec(memory_space=pltpu.VMEM),
        ],
        out_specs=pl.BlockSpec(memory_space=pltpu.VMEM),
        scratch_shapes=[pltpu.VMEM((BUB * CHIPS, LANES), F32)],
    )(boxes, markers.reshape(-1, LANES))


def step_of(j):
    k = j // 4
    m = 4 - (k + 1) // 2
    dy = lax.rem(m + (1 - lax.rem(k, 2)) * (8 - 2 * m), NY)
    dx = lax.rem(lax.rem(j, 4) + 1, NX)
    return dx, dy


def exchange_kernel(
    x_ref,
    p_ref,
    markers,
    velocity,
    adv,
    force,
    x_all,
    pall,
    fbuf,
    nbuf,
    g,
    ssend,
    srecv,
    mhalo,
    vhalo,
    x_send,
    x_recv,
    xs_sem,
    p_send,
    p_recv,
    ps_send,
    ps_recv,
    s_send,
    s_recv,
    h_send,
    h_recv,
):
    gx = lax.axis_index("gx")
    gy = lax.axis_index("gy")
    gz = lax.axis_index("gz")
    y = gz // 2
    c = lax.rem(gz, 2)
    h = y * NX + gy
    other = 1 - c
    sibling = (gx, gy, y * 2 + other)
    up = (lax.rem(gx + 1, NZ), gy, gz)
    down = (lax.rem(gx + NZ - 1, NZ), gy, gz)

    def target(j):
        dx, dy = step_of(j)
        ty, tx = lax.rem(y + dy, NY), lax.rem(gy + dx, NX)
        return ty * NX + tx, (gx, tx, ty * 2 + c)

    def source(j):
        dx, dy = step_of(j)
        ty, tx = lax.rem(y + NY - dy, NY), lax.rem(gy + NX - dx, NX)
        return ty * NX + tx

    barrier = pltpu.get_barrier_semaphore()

    def greet(j, _):
        pl.semaphore_signal(barrier, inc=1, device_id=target(j)[1], device_id_type=MESH)
        return 0

    lax.fori_loop(0, CHIPS - 1, greet, 0)
    for device in (sibling, up, down):
        pl.semaphore_signal(barrier, inc=1, device_id=device, device_id_type=MESH)
    pl.semaphore_wait(barrier, CHIPS - 1 + 3)

    def x_copy(to, device):
        return pltpu.make_async_remote_copy(
            src_ref=x_ref,
            dst_ref=x_all.at[c * CHIPS + h],
            send_sem=x_send.at[to],
            recv_sem=x_recv.at[h],
            device_id=device,
            device_id_type=MESH,
        )

    def p_copy(to, device):
        return pltpu.make_async_remote_copy(
            src_ref=p_ref.at[to],
            dst_ref=pall.at[c * CHIPS + h],
            send_sem=p_send.at[to],
            recv_sem=p_recv.at[h],
            device_id=device,
            device_id_type=MESH,
        )

    def s_copy(to, device):
        return pltpu.make_async_remote_copy(
            src_ref=ssend.at[to],
            dst_ref=srecv.at[h],
            send_sem=s_send.at[to],
            recv_sem=s_recv.at[h],
            device_id=device,
            device_id_type=MESH,
        )

    def x_landed(frm):
        return pltpu.make_async_remote_copy(
            src_ref=x_ref,
            dst_ref=x_all.at[c * CHIPS + frm],
            send_sem=x_send.at[frm],
            recv_sem=x_recv.at[frm],
            device_id=sibling,
            device_id_type=MESH,
        )

    def p_landed(frm):
        return pltpu.make_async_remote_copy(
            src_ref=p_ref.at[frm],
            dst_ref=pall.at[c * CHIPS + frm],
            send_sem=p_send.at[frm],
            recv_sem=p_recv.at[frm],
            device_id=sibling,
            device_id_type=MESH,
        )

    def s_landed(frm):
        return pltpu.make_async_remote_copy(
            src_ref=ssend.at[frm],
            dst_ref=srecv.at[frm],
            send_sem=s_send.at[frm],
            recv_sem=s_recv.at[frm],
            device_id=sibling,
            device_id_type=MESH,
        )

    halos = []
    for way, device, plane in ((0, up, 7), (1, down, 0)):
        halos.append(
            pltpu.make_async_remote_copy(
                src_ref=markers.at[:, plane],
                dst_ref=mhalo.at[way],
                send_sem=h_send.at[2 * way],
                recv_sem=h_recv.at[2 * way],
                device_id=device,
                device_id_type=MESH,
            )
        )
        halos.append(
            pltpu.make_async_remote_copy(
                src_ref=velocity.at[plane],
                dst_ref=vhalo.at[way],
                send_sem=h_send.at[2 * way + 1],
                recv_sem=h_recv.at[2 * way + 1],
                device_id=device,
                device_id_type=MESH,
            )
        )

    def send_x(j, _):
        x_copy(*target(j)).start()
        return 0

    def send_p(j, _):
        p_copy(*target(j)).start()
        return 0

    lax.fori_loop(0, CHIPS - 1, send_x, 0)
    lax.fori_loop(0, CHIPS - 1, send_p, 0)
    for copy in halos:
        copy.start()
    x_all[c * CHIPS + h] = x_ref[...]
    pall[c * CHIPS + h] = p_ref[h]

    def wait_x(j, _):
        x_landed(source(j)).wait_recv()
        return 0

    lax.fori_loop(0, CHIPS - 1, wait_x, 0)
    x_share = pltpu.make_async_remote_copy(
        src_ref=x_all.at[pl.ds(c * CHIPS, CHIPS)],
        dst_ref=x_all.at[pl.ds(c * CHIPS, CHIPS)],
        send_sem=xs_sem.at[0],
        recv_sem=xs_sem.at[1],
        device_id=sibling,
        device_id_type=MESH,
    )
    x_share.start()

    for copy in halos:
        copy.wait()
    low = jnp.where(gx == 0, 0.0, 1.0).astype(F32)
    high = jnp.where(gx == NZ - 1, 0.0, 1.0).astype(F32)

    def advect(t, _):
        rows = pl.ds(pl.multiple_of(t * 8, 8), 8)
        vel = [vhalo[0, rows, :] * low] + [velocity[i, rows, :] for i in range(8)]
        vel = vel + [vhalo[1, rows, :] * high]
        face = [0.5 * (vel[i] + vel[i + 1]) for i in range(9)]
        for m in range(4):
            mark = [mhalo[0, m, rows, :] * low] + [markers[m, i, rows, :] for i in range(8)]
            mark = mark + [mhalo[1, m, rows, :] * high]
            flux = [face[i] * jnp.where(face[i] > 0, mark[i], mark[i + 1]) for i in range(9)]
            for i in range(8):
                here = mark[i + 1]
                adv[m, i, rows, :] = (
                    here - (flux[i + 1] - flux[i]) + here * (face[i + 1] - face[i])
                )
        return 0

    lax.fori_loop(0, 8, advect, 0)

    x_share.wait()

    picks = jnp.where(c == 0, x_all[:, 0, :], x_all[:, 1, :]).astype(BF16)
    row = lax.broadcasted_iota(jnp.int32, (512, LANES), 0)
    lane = lax.broadcasted_iota(jnp.int32, (512, LANES), 1)
    spread = (row // 16 == lane // 4) & (lax.rem(row, 4) == lax.rem(lane, 4))
    wide = lax.dot_general(
        spread.astype(F32).astype(BF16),
        picks,
        (((1,), (1,)), ((), ())),
        preferred_element_type=F32,
    )
    row = lax.broadcasted_iota(jnp.int32, (512, 2 * CHIPS), 0)
    lane = lax.broadcasted_iota(jnp.int32, (512, 2 * CHIPS), 1)
    place = lane - lax.rem(row // 4, 4)
    ones = jnp.ones((2 * CHIPS, 4 * BUB), BF16)
    row = lax.broadcasted_iota(jnp.int32, (512, 4 * BUB), 0)
    lane = lax.broadcasted_iota(jnp.int32, (512, 4 * BUB), 1)
    wanted = (lane - BUB * lax.rem(row // 4, 4)).astype(F32)

    def gather_matrix(k, _):
        mine = jnp.where(place == 4 * k, wide, 0.0).astype(BF16)
        index = jnp.dot(mine, ones, preferred_element_type=F32)
        fbuf[k] = jnp.where(index == wanted, 1.0, 0.0).astype(BF16)
        return 0

    lax.fori_loop(0, 2 * NY, gather_matrix, 0)

    bubble = lax.broadcasted_iota(jnp.int32, (BUB, LANES), 0).astype(F32)
    first = lax.rem(lax.broadcasted_iota(jnp.int32, (1, LANES), 1), 4) < 2

    def sum_matrix(q, _):
        for core in range(2):
            index = x_all[c * CHIPS + q, pl.ds(core, 1), :]
            index = jnp.where(first, pltpu.roll(index, LANES - 2, 1), pltpu.roll(index, 2, 1))
            nbuf[q, :, core * LANES : (core + 1) * LANES] = jnp.where(
                bubble == index, 1.0, 0.0
            ).astype(BF16)
        return 0

    lax.fori_loop(0, CHIPS, sum_matrix, 0)

    def gather(block):
        patches = pall[pl.ds(block * 4, 4)].reshape(4 * BUB, LANES)
        partner = jnp.dot(fbuf[block], patches, preferred_element_type=F32)
        g[:, pl.ds(pl.multiple_of(block * 16, 16), 16), :] = partner.reshape(
            CHIPS, 16, LANES
        ).astype(BF16)

    def share(core, line):
        chips = pl.ds(core * CHIPS + line * 4, 4)
        return pltpu.make_async_remote_copy(
            src_ref=pall.at[chips],
            dst_ref=pall.at[chips],
            send_sem=ps_send.at[line],
            recv_sem=ps_recv.at[line],
            device_id=sibling,
            device_id_type=MESH,
        )

    def line_of(k):
        return source(4 * k) // NX

    def own_line(k, _):
        line = line_of(k)

        def wait_p(j, _):
            p_landed(source(j)).wait_recv()
            return 0

        lax.fori_loop(4 * k, lax.min(4 * k + 4, CHIPS - 1), wait_p, 0)
        share(c, line).start()
        gather(c * NY + line)
        return 0

    lax.fori_loop(0, NY, own_line, 0)

    def other_line(k, _):
        line = line_of(k)
        share(other, line).wait_recv()
        gather(other * NY + line)
        return 0

    lax.fori_loop(0, NY, other_line, 0)

    def sums(q):
        return jnp.dot(nbuf[q], g[q], preferred_element_type=F32).astype(BF16)

    def send_s(j, _):
        to, device = target(j)
        ssend[to] = sums(to)
        s_copy(to, device).start()
        return 0

    lax.fori_loop(0, CHIPS - 1, send_s, 0)
    srecv[h] = sums(h)

    def finish(at):
        patch = p_ref[at].astype(F32)
        lanes = pl.ds(pl.multiple_of(at * LANES, LANES), LANES)
        force[:, lanes] = 0.8 * patch * (1.0 - patch) * srecv[at].astype(F32)

    finish(h)

    def wait_s(j, _):
        frm = source(j)
        s_landed(frm).wait_recv()
        finish(frm)
        return 0

    lax.fori_loop(0, CHIPS - 1, wait_s, 0)

    def wait_sent(j, _):
        to, device = target(j)
        x_copy(to, device).wait_send()
        p_copy(to, device).wait_send()
        s_copy(to, device).wait_send()
        return 0

    lax.fori_loop(0, CHIPS - 1, wait_sent, 0)

    def wait_shared(line, _):
        share(c, line).wait_send()
        return 0

    lax.fori_loop(0, NY, wait_shared, 0)


def exchange(x, patches, markers, velocity):
    vmem = pl.BlockSpec(memory_space=pltpu.VMEM)
    dma = pltpu.SemaphoreType.DMA
    return pl.pallas_call(
        exchange_kernel,
        out_shape=(
            jax.ShapeDtypeStruct(markers.shape, F32),
            jax.ShapeDtypeStruct((BUB, CHIPS * LANES), F32),
        ),
        in_specs=[vmem] * 4,
        out_specs=[vmem] * 2,
        scratch_shapes=[
            pltpu.VMEM((2 * CHIPS, 2, LANES), F32),
            pltpu.VMEM((2 * CHIPS, BUB, LANES), BF16),
            pltpu.VMEM((2 * NY, 512, 4 * BUB), BF16),
            pltpu.VMEM((CHIPS, BUB, 2 * LANES), BF16),
            pltpu.VMEM((CHIPS, 4 * BUB, LANES), BF16),
            pltpu.VMEM((CHIPS, BUB, LANES), BF16),
            pltpu.VMEM((CHIPS, BUB, LANES), BF16),
            pltpu.VMEM((2, 4, 64, LANES), F32),
            pltpu.VMEM((2, 64, LANES), F32),
            dma((CHIPS,)),
            dma((CHIPS,)),
            dma((2,)),
            dma((CHIPS,)),
            dma((CHIPS,)),
            dma((NY,)),
            dma((NY,)),
            dma((CHIPS,)),
            dma((CHIPS,)),
            dma((4,)),
            dma((4,)),
        ],
        compiler_params=pltpu.CompilerParams(
            collective_id=0, has_side_effects=True, vmem_limit_bytes=40 * 1024 * 1024
        ),
    )(x, patches, markers, velocity)


def on_device(markers, velocity, patch_boxes, send_pick, recv_pick, pair_count):
    slots = send_pick.shape[-1]
    used = jnp.arange(slots, dtype=jnp.int32) < pair_count[..., None]
    sent = jnp.where(used, send_pick.astype(F32), UNUSED)
    x = jnp.concatenate([sent, recv_pick.astype(F32)], axis=-1)
    x = x.reshape(NX, NY, 2, 2 * slots).transpose(2, 1, 0, 3).reshape(2, LANES)
    patches = cut(patch_boxes, markers)
    return exchange(x, patches, markers, velocity)


def solution(mesh):
    placed = (
        P(None, "gx", "gy", "gz"),
        P("gx", "gy", "gz"),
        P(None, ("gx", "gy", "gz")),
        P("gx", "gy", "gz", None, None),
        P("gx", "gy", "gz", None, None),
        P("gx", "gy", "gz", None),
    )
    return jax.shard_map(
        on_device,
        mesh=mesh,
        in_specs=placed,
        out_specs=(P(None, "gx", "gy", "gz"), P(("gx", "gy", "gz"), None)),
        check_vma=False,
    )
```

time: 114 us -> 69.6 us (0.61)
  Pallas kernels: 0 us -> 64.1 us
  waiting for transfers between devices: 50.9 us -> 0 us
  starting transfers between devices: 24.6 us -> 0 us
  matrix products: 21.3 us -> 0 us
  local copies, waits for them, and re-layouts: 12.6 us -> 3.22 us
  other arithmetic: 2.83 us -> 1.46 us
    pallas_call x0 -> x2, Pallas kernels: none -> 64.1 us  [the longest x1 55.3 us: exchange(): pl.pallas_call(exchange_kernel, out_shape=(jax.ShapeDtypeStruct(markers.s...]
    all_to_all x2 -> x0, waiting for transfers between devices: 46.6 us -> none  [the longest x1 28.2 us: on_device(): lax.all_to_all(outgoing.reshape(peer_count, slot_count, FLAT), ('gy', 'gz...]
    all_to_all x2 -> x0, starting transfers between devices: 22 us -> none  [the longest x1 15.4 us: on_device(): lax.all_to_all(outgoing.reshape(peer_count, slot_count, FLAT), ('gy', 'gz...]
    dot_general x7 -> x0, matrix products: 21.3 us -> none  [the longest x1 10.7 us: cut_table(): jnp.einsum('bkyz,bpy->bkpz', planes, y_sel, precision=high, preferred_ele...]
    reshape x3 -> x1, local copies, waits for them, and re-layouts: 5.59 us -> 0.11 us  [on_device(): x = x.reshape(NX, NY, 2, 2 * slots).transpose(2, 1, 0, 3).reshape(2, LANES)]
    ppermute x2 -> x0, waiting for transfers between devices: 4.28 us -> none  [the longest x1 4.12 us: extended(): after = lax.ppermute(initial, axis, down)]
    convert_element_type x2 -> x0, local copies, waits for them, and re-layouts: 3.61 us -> none  [the longest x1 2.25 us: cut_table(): return window.reshape(bubble_count, FLAT).astype(jnp.bfloat16)]
    ppermute x2 -> x0, starting transfers between devices: 2.59 us -> none  [the longest x1 1.29 us: extended(): before = lax.ppermute(last, axis, up)]
  transfers between devices with their start and end apart: 4 -> 0, of which waited for: 4 -> 0; matrix products, arithmetic and copies ran while one was open for 2% -> 0% of each run, Pallas kernels for 0% -> 0%
where the time goes in v1:
time: 69.6 us; the launch traced here: 69.4 us
  Pallas kernels  64.1 us (92%)
  local copies, waits for them, and re-layouts  3.22 us (5%)
  other arithmetic  1.46 us (2%)
    pallas_call x1, Pallas kernels, exchange(): pl.pallas_call(exchange_kernel, out_shape=(jax.ShapeDtypeStruct(markers.s...  55.3 us
    pallas_call x1, Pallas kernels, cut(): pl.pallas_call(cut_kernel, out_shape=jax.ShapeDtypeStruct((CHIPS, BUB, LA...  8.8 us
    unnamed x8, local copies, waits for them, and re-layouts  2.99 us

profile of v1, /device:TPU:1, one launch (start us, length us, event | category | flops | bytes accessed | tf_op | source)
XLA Modules:
  0.0 69.4 jit_solution(10207576958348591552)
XLA Ops:
  0.6 0.0 copy-start
  0.6 0.8 %compare_select_fusion = f32[1,1,1,64,2]{3,4,2,1,0:T(2,128)S(1)} fusion(s32[1,1,1,64,2]{3,4,2,1,0:T(2,128)} %param.9, s32[64]{0:T(128)} %bitcast.7), kind=kLoop, calls=%fused_computation.1 | loop fusion | flops 384 | bytes 1280 | tf_op jit(solution)/shard_map/jit(_where)/select_n | solution.py:433
  1.4 0.7 convert_element_type.7
  2.1 0.1 copy.9
  2.2 0.1 reshape.53.x_ref
  2.3 0.0 copy-start.2
  2.3 8.8 %shard_map.80.p_ref = bf16[32,64,128]{2,1,0:T(8,128)(2,1)} custom-call(s32[4,64]{1,0:T(4,128)} %boxes.1, f32[2048,128]{1,0:T(8,128)} %bitcast.5), custom_call_target="tpu_custom_call" | custom-call | tf_op jit(solution)/shard_map/pallas_call | solution.py:47
  11.1 0.0 copy-done
  11.1 0.0 copy-done.2
  11.2 0.0 copy-start.1
  11.2 1.0 %copy-done.1 = bf16[32,64,128]{2,1,0:T(8,128)(2,1)S(1)} copy-done((bf16[32,64,128]{2,1,0:T(8,128)(2,1)S(1)}, bf16[32,64,128]{2,1,0:T(8,128)(2,1)}, u32[]{:S(2)}) %copy-start.1) | copy-done | bytes 524312
  12.2 55.3 %shard_map.81 = (f32[4,8,64,128]{3,2,1,0:T(8,128)S(1)}, f32[64,4096]{1,0:T(8,128)S(1)}) custom-call(f32[2,128]{1,0:T(2,128)S(1)} %reshape.53.x_ref, bf16[32,64,128]{2,1,0:T(8,128)(2,1)S(1)} %copy-done.1, f32[4,8,64,128]{3,2,1,0:T(8,128)S(1)} %copy-done, f32[8,64,128]{2,1,0:T(8,128)S(1)} %copy-done.2), custom_call_target="tpu_custom_call" | custom-call | tf_op jit(solution)/shard_map/pallas_call | solution.py:394
  67.5 1.0 %copy.13 = f32[4,8,64,128]{3,2,1,0:T(8,128)} copy(f32[4,8,64,128]{3,2,1,0:T(8,128)S(1)} %get-tuple-element.4) | data formatting | bytes 2097152
  68.4 1.0 %copy.14 = f32[64,4096]{1,0:T(8,128)} copy(f32[64,4096]{1,0:T(8,128)S(1)} %get-tuple-element.5) | data formatting | bytes 2097152
  (2 shorter events, 0.0 us)
Async XLA Ops:
  0.6 10.5 %copy-start = (f32[4,8,64,128]{3,2,1,0:T(8,128)S(1)}, f32[4,8,64,128]{3,2,1,0:T(8,128)}, u32[]{:S(2)}) copy-start(f32[4,8,64,128]{3,2,1,0:T(8,128)} %markers.1) | copy-start | bytes 3145732
  2.3 8.8 %copy-start.2 = (f32[8,64,128]{2,1,0:T(8,128)S(1)}, f32[8,64,128]{2,1,0:T(8,128)}, u32[]{:S(2)}) copy-start(f32[8,64,128]{2,1,0:T(8,128)} %velocity.1) | copy-start | bytes 786436
  11.2 1.0 %copy-start.1 = (bf16[32,64,128]{2,1,0:T(8,128)(2,1)S(1)}, bf16[32,64,128]{2,1,0:T(8,128)(2,1)}, u32[]{:S(2)}) copy-start(bf16[32,64,128]{2,1,0:T(8,128)(2,1)} %shard_map.80.p_ref) | copy-start | bytes 1572868

commit v2 on v1

v2 whole, which is shorter than its diff:
```python
import jax
import jax.numpy as jnp
from jax import lax
from jax.experimental import pallas as pl
from jax.experimental.pallas import tpu as pltpu
from jax.sharding import PartitionSpec as P

MESH = pl.DeviceIdType.MESH
PATCH = 32
BUB = 64
NY = 8
NX = 4
NZ = 12
CHIPS = NX * NY
HALF = CHIPS // 2
PAIRS = CHIPS
LANES = 128
UNUSED = 512.0
F32 = jnp.float32
BF16 = jnp.bfloat16


def iota(shape, dim):
    return lax.broadcasted_iota(jnp.int32, shape, dim)


def chip_at(h):
    y = lax.rem(h, HALF) // 2
    return 2 * lax.rem(h, 2) + lax.rem(h // HALF + y, 2), y


def peer_at(h, core):
    gy, y = chip_at(h)
    return gy * 16 + y * 2 + core


def exchange_kernel(
    boxes_hbm,
    send_hbm,
    recv_hbm,
    count_hbm,
    markers_hbm,
    velocity_hbm,
    adv,
    force,
    boxes,
    send_pick,
    recv_pick,
    count,
    markers,
    velocity,
    tmp,
    ploc,
    x_msg,
    x_all,
    pall,
    fbuf,
    nidx,
    nbuf,
    g,
    ssend,
    srecv,
    mhalo,
    vhalo,
    in_sem,
    x_send,
    x_recv,
    xs_sem,
    p_send,
    p_recv,
    ps_send,
    ps_recv,
    s_send,
    s_recv,
    h_send,
    h_recv,
):
    gx = lax.axis_index("gx")
    gy = lax.axis_index("gy")
    gz = lax.axis_index("gz")
    y = gz // 2
    c = lax.rem(gz, 2)
    parity = lax.rem(gy + y, 2)
    h = parity * HALF + y * 2 + gy // 2
    other = 1 - c
    sibling = (gx, gy, y * 2 + other)
    up = (lax.rem(gx + 1, NZ), gy, gz)
    down = (lax.rem(gx + NZ - 1, NZ), gy, gz)

    loads = []
    for src, dst in (
        (boxes_hbm, boxes),
        (send_hbm, send_pick),
        (recv_hbm, recv_pick),
        (count_hbm, count),
        *((markers_hbm.at[m], markers.at[m]) for m in range(4)),
        (velocity_hbm, velocity),
    ):
        loads.append(pltpu.make_async_copy(src, dst, in_sem.at[len(loads)]))
        loads[-1].start()

    def row_step(k):
        m = 4 - (k + 1) // 2
        return lax.rem(m + (1 - lax.rem(k, 2)) * (8 - 2 * m), NY)

    def place(dx, dy):
        ty, tx = lax.rem(y + dy, NY), lax.rem(gy + dx, NX)
        number = lax.rem(tx + ty, 2) * HALF + ty * 2 + tx // 2
        return number, (gx, tx, ty * 2 + c)

    def target(j):
        return place(lax.rem(lax.rem(j, 4) + 1, NX), row_step(j // 4))

    def target_in(half, i):
        dy = row_step(i // 2)
        turn = lax.rem(half + parity + dy, 2)
        dx = turn + 2 * (1 - lax.rem(i, 2))
        return place(lax.rem(dx, NX), dy)

    barrier = pltpu.get_barrier_semaphore()

    def greet(j, _):
        pl.semaphore_signal(barrier, inc=1, device_id=target(j)[1], device_id_type=MESH)
        return 0

    lax.fori_loop(0, CHIPS - 1, greet, 0)
    for device in (sibling, up, down):
        pl.semaphore_signal(barrier, inc=1, device_id=device, device_id_type=MESH)

    for copy in loads:
        copy.wait()

    for s in range(2):
        far = jnp.where(count[...] > s, send_pick[s : s + 1, :].astype(F32), UNUSED)
        x_msg[s : s + 1, 0:BUB] = far
        x_msg[s : s + 1, BUB:LANES] = recv_pick[s : s + 1, :].astype(F32)

    group = iota((8, LANES), 1) // PATCH
    rows = markers.reshape(4 * 8 * 64, LANES)

    def cut(half):
        def one(b, _):
            base = (boxes[0, b] * 8 + boxes[1, b]) * 64 + boxes[2, b]
            z0 = boxes[3, b]
            for dx in range(2):
                cells = None
                for j in range(4):
                    piece = rows[pl.ds(base + (2 * half + dx) * 64 + j, 8, stride=4), :]
                    piece = pltpu.roll(piece, lax.rem(PATCH * j - z0 + LANES, LANES), 1)
                    cells = piece if j == 0 else jnp.where(group == j, piece, cells)
                tmp[pl.ds(pl.multiple_of(b * HALF + dx * 8, 8), 8), :] = cells
            return 0

        lax.fori_loop(0, BUB, one, 0, unroll=8)

        def put(s, _):
            ploc[half * HALF + s] = tmp[pl.ds(s, BUB, stride=HALF), :].astype(BF16)
            return 0

        lax.fori_loop(0, HALF, put, 0, unroll=4)

    cut(0)

    pl.semaphore_wait(barrier, CHIPS - 1 + 3)

    def x_copy(to, device):
        return pltpu.make_async_remote_copy(
            src_ref=x_msg,
            dst_ref=x_all.at[c * CHIPS + h],
            send_sem=x_send.at[to],
            recv_sem=x_recv.at[h],
            device_id=device,
            device_id_type=MESH,
        )

    def p_copy(to, device):
        return pltpu.make_async_remote_copy(
            src_ref=ploc.at[to],
            dst_ref=pall.at[c * CHIPS + h],
            send_sem=p_send.at[to],
            recv_sem=p_recv.at[h],
            device_id=device,
            device_id_type=MESH,
        )

    def s_copy(to, device):
        return pltpu.make_async_remote_copy(
            src_ref=ssend.at[to],
            dst_ref=srecv.at[h],
            send_sem=s_send.at[to],
            recv_sem=s_recv.at[h],
            device_id=device,
            device_id_type=MESH,
        )

    def landed(buffer, at, send_sem, recv_sem, frm):
        return pltpu.make_async_remote_copy(
            src_ref=buffer.at[at],
            dst_ref=buffer.at[at],
            send_sem=send_sem.at[frm],
            recv_sem=recv_sem.at[frm],
            device_id=sibling,
            device_id_type=MESH,
        )

    halos = []
    for way, device, plane in ((0, up, 7), (1, down, 0)):
        halos.append(
            pltpu.make_async_remote_copy(
                src_ref=markers.at[:, plane],
                dst_ref=mhalo.at[way],
                send_sem=h_send.at[2 * way],
                recv_sem=h_recv.at[2 * way],
                device_id=device,
                device_id_type=MESH,
            )
        )
        halos.append(
            pltpu.make_async_remote_copy(
                src_ref=velocity.at[plane],
                dst_ref=vhalo.at[way],
                send_sem=h_send.at[2 * way + 1],
                recv_sem=h_recv.at[2 * way + 1],
                device_id=device,
                device_id_type=MESH,
            )
        )

    def send_half(half):
        def send(i, _):
            to, device = target_in(half, i)
            x_copy(to, device).start()
            p_copy(to, device).start()
            return 0

        lax.fori_loop(0, jnp.where(parity == half, HALF - 1, HALF), send, 0)

    send_half(0)
    cut(1)
    send_half(1)
    for copy in halos:
        copy.start()
    x_all[c * CHIPS + h] = x_msg[...]
    pall[c * CHIPS + h] = ploc[h]

    def wait_x(j, _):
        frm = target(j)[0]
        landed(x_all, c * CHIPS + frm, x_send, x_recv, frm).wait_recv()
        return 0

    lax.fori_loop(0, CHIPS - 1, wait_x, 0)
    x_share = pltpu.make_async_remote_copy(
        src_ref=x_all.at[pl.ds(c * CHIPS, CHIPS)],
        dst_ref=x_all.at[pl.ds(c * CHIPS, CHIPS)],
        send_sem=xs_sem.at[0],
        recv_sem=xs_sem.at[1],
        device_id=sibling,
        device_id_type=MESH,
    )
    x_share.start()

    row = iota((256, LANES), 0)
    lane = iota((256, LANES), 1)
    from_peer = peer_at(row // 8, c)
    slot = lax.rem(row, 4)
    spread = []
    for s in range(2):
        hit = (lax.rem(slot, 2) == s) & (lane == from_peer + jnp.where(slot < 2, 0, BUB))
        spread.append(jnp.where(hit, 1.0, 0.0).astype(BF16))
    wanted = (lane - BUB * lax.rem(row // 4, 2)).astype(F32)

    row = iota((LANES, 256), 0)
    lane = iota((LANES, 256), 1)
    to_peer = peer_at(lax.rem(lane // 4, CHIPS), lane // LANES)
    slot = lax.rem(lane, 4)
    order = []
    for s in range(2):
        hit = (lax.rem(slot, 2) == s) & (row == to_peer + jnp.where(slot < 2, BUB, 0))
        order.append(jnp.where(hit, 1.0, 0.0).astype(BF16))

    x_share.wait()

    wide = jnp.zeros((256, 2 * CHIPS), F32)
    index = jnp.zeros((CHIPS, 256), F32)
    for s in range(2):
        wide += lax.dot_general(
            spread[s],
            x_all[:, s, :].astype(BF16),
            (((1,), (1,)), ((), ())),
            preferred_element_type=F32,
        )
        index += jnp.dot(
            x_all[pl.ds(c * CHIPS, CHIPS), s, :].astype(BF16),
            order[s],
            preferred_element_type=F32,
        )
    nidx[...] = index
    row = iota((256, 2 * CHIPS), 0)
    lane = iota((256, 2 * CHIPS), 1)
    wide = jnp.where(lax.rem(lane, 2) == lax.rem(row // 4, 2), wide, 0.0).astype(BF16)
    pair_of = iota((2 * CHIPS, LANES), 0) // 2

    def gather_matrix(k, _):
        pick = jnp.where(pair_of == k, 1.0, 0.0).astype(BF16)
        index = jnp.dot(wide, pick, preferred_element_type=F32)
        fbuf[k] = jnp.where(index == wanted, 1.0, 0.0).astype(BF16)
        return 0

    lax.fori_loop(0, PAIRS, gather_matrix, 0, unroll=2)

    bubble = iota((BUB, 2 * LANES), 0).astype(F32)

    def sum_matrix(q, _):
        nbuf[q] = jnp.where(bubble == nidx[pl.ds(q, 1), :], 1.0, 0.0).astype(BF16)
        return 0

    lax.fori_loop(0, CHIPS, sum_matrix, 0, unroll=4)

    def gather(line):
        for i in range(2):
            pair = 2 * line + i
            patches = pall[pl.ds(2 * pair, 2)].reshape(2 * BUB, LANES)
            partner = jnp.dot(fbuf[pair], patches, preferred_element_type=F32)
            g[:, pl.ds(pl.multiple_of(pair * 8, 8), 8), :] = partner.reshape(CHIPS, 8, LANES)

    def share(core, line):
        chips = pl.ds(core * CHIPS + line * 4, 4)
        return pltpu.make_async_remote_copy(
            src_ref=pall.at[chips],
            dst_ref=pall.at[chips],
            send_sem=ps_send.at[line],
            recv_sem=ps_recv.at[line],
            device_id=sibling,
            device_id_type=MESH,
        )

    def line_of(k):
        return (k // 4) * 4 + lax.rem(y // 2 + 2 + 3 * lax.rem(k, 4), 4)

    def own_line(k, _):
        line = line_of(k)

        def wait_p(i, _):
            frm = line * 4 + i

            @pl.when(frm != h)
            def _():
                landed(pall, c * CHIPS + frm, p_send, p_recv, frm).wait_recv()

            return 0

        lax.fori_loop(0, 4, wait_p, 0)
        share(c, line).start()
        gather(c * NY + line)
        return 0

    lax.fori_loop(0, NY, own_line, 0)

    def other_line(k, _):
        line = line_of(k)
        share(other, line).wait_recv()
        gather(other * NY + line)
        return 0

    lax.fori_loop(0, NY, other_line, 0)

    def sums(q):
        return jnp.dot(nbuf[q], g[q].astype(BF16), preferred_element_type=F32).astype(BF16)

    def send_s(j, _):
        to, device = target(j)
        ssend[to] = sums(to)
        s_copy(to, device).start()
        return 0

    lax.fori_loop(0, CHIPS - 1, send_s, 0)
    srecv[h] = sums(h)

    for copy in halos:
        copy.wait()
    low = jnp.where(gx == 0, 0.0, 1.0).astype(F32)
    high = jnp.where(gx == NZ - 1, 0.0, 1.0).astype(F32)

    def advect(t, _):
        rows = pl.ds(pl.multiple_of(t * 8, 8), 8)
        vel = [vhalo[0, rows, :] * low] + [velocity[i, rows, :] for i in range(8)]
        vel = vel + [vhalo[1, rows, :] * high]
        face = [0.5 * (vel[i] + vel[i + 1]) for i in range(9)]
        for m in range(4):
            mark = [mhalo[0, m, rows, :] * low] + [markers[m, i, rows, :] for i in range(8)]
            mark = mark + [mhalo[1, m, rows, :] * high]
            flux = [face[i] * jnp.where(face[i] > 0, mark[i], mark[i + 1]) for i in range(9)]
            for i in range(8):
                here = mark[i + 1]
                adv[m, i, rows, :] = (
                    here - (flux[i + 1] - flux[i]) + here * (face[i + 1] - face[i])
                )
        return 0

    lax.fori_loop(0, 8, advect, 0)

    def finish(at):
        patch = ploc[at].astype(F32)
        lanes = pl.ds(pl.multiple_of(at * LANES, LANES), LANES)
        force[:, lanes] = 0.8 * patch * (1.0 - patch) * srecv[at].astype(F32)

    finish(h)

    def wait_s(j, _):
        frm = target(j)[0]
        landed(srecv, frm, s_send, s_recv, frm).wait_recv()
        finish(frm)
        return 0

    lax.fori_loop(0, CHIPS - 1, wait_s, 0)

    def wait_sent(j, _):
        to, device = target(j)
        x_copy(to, device).wait_send()
        p_copy(to, device).wait_send()
        s_copy(to, device).wait_send()
        return 0

    lax.fori_loop(0, CHIPS - 1, wait_sent, 0)

    def wait_shared(line, _):
        share(c, line).wait_send()
        return 0

    lax.fori_loop(0, NY, wait_shared, 0)


def exchange(boxes, send_pick, recv_pick, count, markers, velocity):
    vmem = pl.BlockSpec(memory_space=pltpu.VMEM)
    hbm = pl.BlockSpec(memory_space=pltpu.HBM)
    dma = pltpu.SemaphoreType.DMA
    return pl.pallas_call(
        exchange_kernel,
        out_shape=(
            pltpu.VMEM(markers.shape, F32),
            pltpu.VMEM((BUB, CHIPS * LANES), F32),
        ),
        in_specs=[hbm] * 6,
        out_specs=[vmem] * 2,
        scratch_shapes=[
            pltpu.SMEM(boxes.shape, jnp.int32),
            pltpu.VMEM(send_pick.shape, jnp.int32),
            pltpu.VMEM(recv_pick.shape, jnp.int32),
            pltpu.VMEM(count.shape, jnp.int32),
            pltpu.VMEM(markers.shape, F32),
            pltpu.VMEM(velocity.shape, F32),
            pltpu.VMEM((BUB * HALF, LANES), F32),
            pltpu.VMEM((CHIPS, BUB, LANES), BF16),
            pltpu.VMEM((2, LANES), F32),
            pltpu.VMEM((2 * CHIPS, 2, LANES), F32),
            pltpu.VMEM((2 * CHIPS, BUB, LANES), BF16),
            pltpu.VMEM((PAIRS, 256, LANES), BF16),
            pltpu.VMEM((CHIPS, 256), F32),
            pltpu.VMEM((CHIPS, BUB, 2 * LANES), BF16),
            pltpu.VMEM((CHIPS, 256, LANES), F32),
            pltpu.VMEM((CHIPS, BUB, LANES), BF16),
            pltpu.VMEM((CHIPS, BUB, LANES), BF16),
            pltpu.VMEM((2, 4, 64, LANES), F32),
            pltpu.VMEM((2, 64, LANES), F32),
            dma((9,)),
            dma((CHIPS,)),
            dma((CHIPS,)),
            dma((2,)),
            dma((CHIPS,)),
            dma((CHIPS,)),
            dma((NY,)),
            dma((NY,)),
            dma((CHIPS,)),
            dma((CHIPS,)),
            dma((4,)),
            dma((4,)),
        ],
        compiler_params=pltpu.CompilerParams(
            collective_id=0, has_side_effects=True, vmem_limit_bytes=60 * 1024 * 1024
        ),
    )(boxes, send_pick, recv_pick, count, markers, velocity)


def write_kernel(adv, force, adv_out, force_out, sem):
    copies = []
    for i in range(4):
        copies.append(pltpu.make_async_copy(adv.at[i], adv_out.at[i], sem.at[i]))
        part = pl.ds(16 * i, 16)
        copies.append(pltpu.make_async_copy(force.at[part], force_out.at[part], sem.at[4 + i]))
    for copy in copies:
        copy.start()
    for copy in copies:
        copy.wait()


def write(adv, force):
    return pl.pallas_call(
        write_kernel,
        out_shape=(
            jax.ShapeDtypeStruct(adv.shape, F32),
            jax.ShapeDtypeStruct(force.shape, F32),
        ),
        in_specs=[pl.BlockSpec(memory_space=pltpu.VMEM)] * 2,
        out_specs=[pl.BlockSpec(memory_space=pl.ANY)] * 2,
        scratch_shapes=[pltpu.SemaphoreType.DMA((8,))],
        compiler_params=pltpu.CompilerParams(vmem_limit_bytes=16 * 1024 * 1024),
    )(adv, force)


def on_device(markers, velocity, patch_boxes, send_pick, recv_pick, pair_count):
    peers, slots = send_pick.shape[-2:]
    adv, force = exchange(
        patch_boxes,
        send_pick.reshape(peers, slots).T,
        recv_pick.reshape(peers, slots).T,
        pair_count.reshape(1, peers),
        markers,
        velocity,
    )
    return tuple(write(adv, force))


def solution(mesh):
    placed = (
        P(None, "gx", "gy", "gz"),
        P("gx", "gy", "gz"),
        P(None, ("gx", "gy", "gz")),
        P("gx", "gy", "gz", None, None),
        P("gx", "gy", "gz", None, None),
        P("gx", "gy", "gz", None),
    )
    return jax.shard_map(
        on_device,
        mesh=mesh,
        in_specs=placed,
        out_specs=(P(None, "gx", "gy", "gz"), P(("gx", "gy", "gz"), None)),
        check_vma=False,
    )
```

time: 69.6 us -> 57.8 us (0.83)
  Pallas kernels: 64.1 us -> 57 us
  local copies, waits for them, and re-layouts: 3.22 us -> 0 us
  other arithmetic: 1.46 us -> 0 us
    pallas_call x2, Pallas kernels: 64.1 us -> 57 us  [the longest x1 55.6 us: exchange(): pl.pallas_call(exchange_kernel, out_shape=(pltpu.VMEM(markers.shape, F32)...]
    unnamed x8 -> x0, local copies, waits for them, and re-layouts: 2.99 us -> none
    select_n x1 -> x0, other arithmetic: 0.77 us -> none  [on_device(): sent = jnp.where(used, send_pick.astype(F32), UNUSED)]
where the time goes in v2:
time: 57.8 us; the launch traced here: 57.6 us
  Pallas kernels  57 us (99%)
  between operations  0.64 us (1%)
    pallas_call x1, Pallas kernels, exchange(): pl.pallas_call(exchange_kernel, out_shape=(pltpu.VMEM(markers.shape, F32)...  55.6 us
    pallas_call x1, Pallas kernels, write(): pl.pallas_call(write_kernel, out_shape=(jax.ShapeDtypeStruct(adv.shape, F...  1.38 us

profile of v2, /device:TPU:1, one launch (start us, length us, event | category | flops | bytes accessed | tf_op | source)
XLA Modules:
  0.0 57.6 jit_solution(18349834675693064538)
XLA Ops:
  0.6 55.6 %shard_map.77 = (f32[4,8,64,128]{3,2,1,0:T(8,128)S(1)}, f32[64,4096]{1,0:T(8,128)S(1)}) custom-call(s32[4,64]{1,0:T(4,128)} %boxes_hbm.1, s32[2,64]{1,0:T(2,128)} %bitcast.7, s32[2,64]{1,0:T(2,128)} %bitcast.8, s32[1,64]{1,0:T(1,128)} %bitcast.9, f32[4,8,64,128]{3,2,1,0:T(8,128)} %markers_hbm.1, f32[8,64,128]{2,1,0:T(8,128)} %velocity_hbm.1), custom_call_target="tpu_custom_call" | custom-call | tf_op jit(solution)/shard_map/pallas_call | solution.py:437
  56.2 1.4 %shard_map.78 = (f32[4,8,64,128]{3,2,1,0:T(8,128)}, f32[64,4096]{1,0:T(8,128)}) custom-call(f32[4,8,64,128]{3,2,1,0:T(8,128)S(1)} %get-tuple-element.4.adv, f32[64,4096]{1,0:T(8,128)S(1)} %get-tuple-element.5.force), custom_call_target="tpu_custom_call" | custom-call | tf_op jit(solution)/shard_map/pallas_call | solution.py:497

commit v3 on v2

--- a/solution.py
+++ b/solution.py
@@ -16,6 +16,7 @@
 PAIRS = CHIPS
 LANES = 128
 UNUSED = 512.0
+ROWS = (4, 3, 5, 2, 6, 1, 7, 0)
 F32 = jnp.float32
 BF16 = jnp.bfloat16
 
@@ -99,31 +100,40 @@
         loads.append(pltpu.make_async_copy(src, dst, in_sem.at[len(loads)]))
         loads[-1].start()
 
-    def row_step(k):
+    ys = [lax.rem(y + dy, NY) for dy in range(NY)]
+    xs = [lax.rem(gy + dx, NX) for dx in range(NX)]
+    base = [[lax.rem(parity + i, 2) * HALF + xs[dx] // 2 for dx in range(NX)] for i in range(2)]
+
+    def place(dx, dy):
+        number = base[(dx + dy) % 2][dx] + ys[dy] * 2
+        return number, (gx, xs[dx], ys[dy] * 2 + c)
+
+    others = [place(dx, dy) for dy in ROWS for dx in (1, 2, 3, 0)][:-1]
+
+    def others_in(half):
+        same = parity == half
+        even = [jnp.where(same, xs[dx], xs[dx + 1]) for dx in (2, 0)]
+        odd = [jnp.where(same, xs[dx + 1], xs[dx]) for dx in (2, 0)]
+        found = []
+        for dy in ROWS:
+            for at in odd if dy % 2 else even:
+                found.append((half * HALF + ys[dy] * 2 + at // 2, (gx, at, ys[dy] * 2 + c)))
+        return found
+
+    def row_of(k):
         m = 4 - (k + 1) // 2
-        return lax.rem(m + (1 - lax.rem(k, 2)) * (8 - 2 * m), NY)
-
-    def place(dx, dy):
-        ty, tx = lax.rem(y + dy, NY), lax.rem(gy + dx, NX)
-        number = lax.rem(tx + ty, 2) * HALF + ty * 2 + tx // 2
-        return number, (gx, tx, ty * 2 + c)
-
-    def target(j):
-        return place(lax.rem(lax.rem(j, 4) + 1, NX), row_step(j // 4))
-
-    def target_in(half, i):
-        dy = row_step(i // 2)
-        turn = lax.rem(half + parity + dy, 2)
-        dx = turn + 2 * (1 - lax.rem(i, 2))
-        return place(lax.rem(dx, NX), dy)
+        ty = lax.rem(y + m + (1 - lax.rem(k, 2)) * (8 - 2 * m), NY)
+        odd = lax.rem(ty - y + NY, 2)
+        row = []
+        for dx in (1, 2, 3, 0):
+            at = lax.rem(parity + odd + dx, 2) * HALF + ty * 2 + xs[dx] // 2
+            row.append((at, (gx, xs[dx], ty * 2 + c)))
+        return row
 
     barrier = pltpu.get_barrier_semaphore()
 
-    def greet(j, _):
-        pl.semaphore_signal(barrier, inc=1, device_id=target(j)[1], device_id_type=MESH)
-        return 0
-
-    lax.fori_loop(0, CHIPS - 1, greet, 0)
+    for _, device in others:
+        pl.semaphore_signal(barrier, inc=1, device_id=device, device_id_type=MESH)
     for device in (sibling, up, down):
         pl.semaphore_signal(barrier, inc=1, device_id=device, device_id_type=MESH)
 
@@ -227,14 +237,16 @@
         )
 
     def send_half(half):
-        def send(i, _):
-            to, device = target_in(half, i)
-            x_copy(to, device).start()
+        found = others_in(half)
+        for to, device in found[:-1]:
             p_copy(to, device).start()
-            return 0
-
-        lax.fori_loop(0, jnp.where(parity == half, HALF - 1, HALF), send, 0)
-
+
+        @pl.when(parity != half)
+        def _():
+            p_copy(*found[-1]).start()
+
+    for to, device in others:
+        x_copy(to, device).start()
     send_half(0)
     cut(1)
     send_half(1)
@@ -243,12 +255,8 @@
     x_all[c * CHIPS + h] = x_msg[...]
     pall[c * CHIPS + h] = ploc[h]
 
-    def wait_x(j, _):
-        frm = target(j)[0]
+    for frm, _ in others:
         landed(x_all, c * CHIPS + frm, x_send, x_recv, frm).wait_recv()
-        return 0
-
-    lax.fori_loop(0, CHIPS - 1, wait_x, 0)
     x_share = pltpu.make_async_remote_copy(
         src_ref=x_all.at[pl.ds(c * CHIPS, CHIPS)],
         dst_ref=x_all.at[pl.ds(c * CHIPS, CHIPS)],
@@ -278,36 +286,40 @@
         hit = (lax.rem(slot, 2) == s) & (row == to_peer + jnp.where(slot < 2, BUB, 0))
         order.append(jnp.where(hit, 1.0, 0.0).astype(BF16))
 
-    x_share.wait()
-
-    wide = jnp.zeros((256, 2 * CHIPS), F32)
+    half_row = iota((256, CHIPS), 0)
+    half_lane = iota((256, CHIPS), 1)
+    pair_half = lax.rem(half_lane, 2) == lax.rem(half_row // 4, 2)
+    pair_of = iota((CHIPS, LANES), 0) // 2
+
+    def gather_matrices(core):
+        wide = jnp.zeros((256, CHIPS), F32)
+        for s in range(2):
+            wide += lax.dot_general(
+                spread[s],
+                x_all[pl.ds(core * CHIPS, CHIPS), s, :].astype(BF16),
+                (((1,), (1,)), ((), ())),
+                preferred_element_type=F32,
+            )
+        wide = jnp.where(pair_half, wide, 0.0).astype(BF16)
+
+        def matrix(k, _):
+            pick = jnp.where(pair_of == k, 1.0, 0.0).astype(BF16)
+            index = jnp.dot(wide, pick, preferred_element_type=F32)
+            fbuf[core * HALF + k] = jnp.where(index == wanted, 1.0, 0.0).astype(BF16)
+            return 0
+
+        lax.fori_loop(0, HALF, matrix, 0, unroll=8)
+
+    gather_matrices(c)
+
     index = jnp.zeros((CHIPS, 256), F32)
     for s in range(2):
-        wide += lax.dot_general(
-            spread[s],
-            x_all[:, s, :].astype(BF16),
-            (((1,), (1,)), ((), ())),
-            preferred_element_type=F32,
-        )
         index += jnp.dot(
             x_all[pl.ds(c * CHIPS, CHIPS), s, :].astype(BF16),
             order[s],
             preferred_element_type=F32,
         )
     nidx[...] = index
-    row = iota((256, 2 * CHIPS), 0)
-    lane = iota((256, 2 * CHIPS), 1)
-    wide = jnp.where(lax.rem(lane, 2) == lax.rem(row // 4, 2), wide, 0.0).astype(BF16)
-    pair_of = iota((2 * CHIPS, LANES), 0) // 2
-
-    def gather_matrix(k, _):
-        pick = jnp.where(pair_of == k, 1.0, 0.0).astype(BF16)
-        index = jnp.dot(wide, pick, preferred_element_type=F32)
-        fbuf[k] = jnp.where(index == wanted, 1.0, 0.0).astype(BF16)
-        return 0
-
-    lax.fori_loop(0, PAIRS, gather_matrix, 0, unroll=2)
-
     bubble = iota((BUB, 2 * LANES), 0).astype(F32)
 
     def sum_matrix(q, _):
@@ -316,9 +328,9 @@
 
     lax.fori_loop(0, CHIPS, sum_matrix, 0, unroll=4)
 
-    def gather(line):
-        for i in range(2):
-            pair = 2 * line + i
+    def gather(core, half):
+        for i in range(8):
+            pair = core * HALF + half * 8 + i
             patches = pall[pl.ds(2 * pair, 2)].reshape(2 * BUB, LANES)
             partner = jnp.dot(fbuf[pair], patches, preferred_element_type=F32)
             g[:, pl.ds(pl.multiple_of(pair * 8, 8), 8), :] = partner.reshape(CHIPS, 8, LANES)
@@ -334,47 +346,51 @@
             device_id_type=MESH,
         )
 
-    def line_of(k):
-        return (k // 4) * 4 + lax.rem(y // 2 + 2 + 3 * lax.rem(k, 4), 4)
-
-    def own_line(k, _):
-        line = line_of(k)
-
-        def wait_p(i, _):
-            frm = line * 4 + i
-
-            @pl.when(frm != h)
-            def _():
-                landed(pall, c * CHIPS + frm, p_send, p_recv, frm).wait_recv()
-
-            return 0
-
-        lax.fori_loop(0, 4, wait_p, 0)
-        share(c, line).start()
-        gather(c * NY + line)
+    def lines(half):
+        return [half * 4 + lax.rem(y // 2 + step, 4) for step in (2, 1, 3, 0)]
+
+    for half in range(2):
+        for line in lines(half):
+            for i in range(4):
+                frm = line * 4 + i
+
+                @pl.when(frm != h)
+                def _():
+                    landed(pall, c * CHIPS + frm, p_send, p_recv, frm).wait_recv()
+
+            share(c, line).start()
+        gather(c, half)
+
+    x_share.wait()
+    gather_matrices(other)
+
+    for half in range(2):
+        for line in lines(half):
+            share(other, line).wait_recv()
+        gather(other, half)
+
+    def send_s(k, _):
+        row = row_of(k)
+        for to, _ in row:
+            part = jnp.dot(nbuf[to], g[to].astype(BF16), preferred_element_type=F32)
+            ssend[to] = part.astype(BF16)
+        for to, device in row[:-1]:
+            s_copy(to, device).start()
+
+        @pl.when(k < NY - 1)
+        def _():
+            s_copy(*row[-1]).start()
+
         return 0
 
-    lax.fori_loop(0, NY, own_line, 0)
-
-    def other_line(k, _):
-        line = line_of(k)
-        share(other, line).wait_recv()
-        gather(other * NY + line)
-        return 0
-
-    lax.fori_loop(0, NY, other_line, 0)
-
-    def sums(q):
-        return jnp.dot(nbuf[q], g[q].astype(BF16), preferred_element_type=F32).astype(BF16)
-
-    def send_s(j, _):
-        to, device = target(j)
-        ssend[to] = sums(to)
-        s_copy(to, device).start()
-        return 0
-
-    lax.fori_loop(0, CHIPS - 1, send_s, 0)
-    srecv[h] = sums(h)
+    lax.fori_loop(0, NY, send_s, 0)
+    srecv[h] = ssend[h]
+
+    for to, device in others:
+        x_copy(to, device).wait_send()
+        p_copy(to, device).wait_send()
+    for line in range(NY):
+        share(c, line).wait_send()
 
     for copy in halos:
         copy.wait()
@@ -404,30 +420,23 @@
         lanes = pl.ds(pl.multiple_of(at * LANES, LANES), LANES)
         force[:, lanes] = 0.8 * patch * (1.0 - patch) * srecv[at].astype(F32)
 
-    finish(h)
-
-    def wait_s(j, _):
-        frm = target(j)[0]
-        landed(srecv, frm, s_send, s_recv, frm).wait_recv()
-        finish(frm)
+    def finish_row(k, _):
+        row = row_of(k)
+        for at, device in row[:-1]:
+            landed(srecv, at, s_send, s_recv, at).wait_recv()
+            s_copy(at, device).wait_send()
+
+        @pl.when(k < NY - 1)
+        def _():
+            at, device = row[-1]
+            landed(srecv, at, s_send, s_recv, at).wait_recv()
+            s_copy(at, device).wait_send()
+
+        for at, _ in row:
+            finish(at)
         return 0
 
-    lax.fori_loop(0, CHIPS - 1, wait_s, 0)
-
-    def wait_sent(j, _):
-        to, device = target(j)
-        x_copy(to, device).wait_send()
-        p_copy(to, device).wait_send()
-        s_copy(to, device).wait_send()
-        return 0
-
-    lax.fori_loop(0, CHIPS - 1, wait_sent, 0)
-
-    def wait_shared(line, _):
-        share(c, line).wait_send()
-        return 0
-
-    lax.fori_loop(0, NY, wait_shared, 0)
+    lax.fori_loop(0, NY, finish_row, 0)
 
 
 def exchange(boxes, send_pick, recv_pick, count, markers, velocity):

time: 57.8 us -> 50.5 us (0.87)
  Pallas kernels: 57 us -> 49.7 us
    pallas_call x1, Pallas kernels: 55.6 us -> 48.3 us  [exchange(): pl.pallas_call(exchange_kernel, out_shape=(pltpu.VMEM(markers.shape, F32)...]
where the time goes in v3:
time: 50.5 us; the launch traced here: 50.3 us
  Pallas kernels  49.7 us (98%)
  between operations  0.64 us (1%)
    pallas_call x1, Pallas kernels, exchange(): pl.pallas_call(exchange_kernel, out_shape=(pltpu.VMEM(markers.shape, F32)...  48.3 us
    pallas_call x1, Pallas kernels, write(): pl.pallas_call(write_kernel, out_shape=(jax.ShapeDtypeStruct(adv.shape, F...  1.38 us

profile of v3, /device:TPU:1, one launch (start us, length us, event | category | flops | bytes accessed | tf_op | source)
XLA Modules:
  0.0 50.3 jit_solution(7691563838380618134)
XLA Ops:
  0.6 48.3 %shard_map.77 = (f32[4,8,64,128]{3,2,1,0:T(8,128)S(1)}, f32[64,4096]{1,0:T(8,128)S(1)}) custom-call(s32[4,64]{1,0:T(4,128)} %boxes_hbm.1, s32[2,64]{1,0:T(2,128)} %bitcast.7, s32[2,64]{1,0:T(2,128)} %bitcast.8, s32[1,64]{1,0:T(1,128)} %bitcast.9, f32[4,8,64,128]{3,2,1,0:T(8,128)} %markers_hbm.1, f32[8,64,128]{2,1,0:T(8,128)} %velocity_hbm.1), custom_call_target="tpu_custom_call" | custom-call | tf_op jit(solution)/shard_map/pallas_call | solution.py:446
  48.9 1.4 %shard_map.78 = (f32[4,8,64,128]{3,2,1,0:T(8,128)}, f32[64,4096]{1,0:T(8,128)}) custom-call(f32[4,8,64,128]{3,2,1,0:T(8,128)S(1)} %get-tuple-element.4.adv, f32[64,4096]{1,0:T(8,128)S(1)} %get-tuple-element.5.force), custom_call_target="tpu_custom_call" | custom-call | tf_op jit(solution)/shard_map/pallas_call | solution.py:506

commit v4 on v3

--- a/solution.py
+++ b/solution.py
@@ -85,8 +85,7 @@
     h = parity * HALF + y * 2 + gy // 2
     other = 1 - c
     sibling = (gx, gy, y * 2 + other)
-    up = (lax.rem(gx + 1, NZ), gy, gz)
-    down = (lax.rem(gx + NZ - 1, NZ), gy, gz)
+    sides = ((gx < NZ - 1, (gx + 1, gy, gz), 7), (gx > 0, (gx - 1, gy, gz), 0))
 
     loads = []
     for src, dst in (
@@ -134,8 +133,13 @@
 
     for _, device in others:
         pl.semaphore_signal(barrier, inc=1, device_id=device, device_id_type=MESH)
-    for device in (sibling, up, down):
-        pl.semaphore_signal(barrier, inc=1, device_id=device, device_id_type=MESH)
+    pl.semaphore_signal(barrier, inc=1, device_id=sibling, device_id_type=MESH)
+    for there, device, _ in sides:
+
+        @pl.when(there)
+        def _():
+            pl.semaphore_signal(barrier, inc=1, device_id=device, device_id_type=MESH)
+
 
     for copy in loads:
         copy.wait()
@@ -171,7 +175,8 @@
 
     cut(0)
 
-    pl.semaphore_wait(barrier, CHIPS - 1 + 3)
+    neighbours = jnp.where(gx < NZ - 1, 1, 0) + jnp.where(gx > 0, 1, 0)
+    pl.semaphore_wait(barrier, CHIPS + neighbours)
 
     def x_copy(to, device):
         return pltpu.make_async_remote_copy(
@@ -213,9 +218,9 @@
             device_id_type=MESH,
         )
 
-    halos = []
-    for way, device, plane in ((0, up, 7), (1, down, 0)):
-        halos.append(
+    def halo_copies(way):
+        _, device, plane = sides[way]
+        return (
             pltpu.make_async_remote_copy(
                 src_ref=markers.at[:, plane],
                 dst_ref=mhalo.at[way],
@@ -223,9 +228,7 @@
                 recv_sem=h_recv.at[2 * way],
                 device_id=device,
                 device_id_type=MESH,
-            )
-        )
-        halos.append(
+            ),
             pltpu.make_async_remote_copy(
                 src_ref=velocity.at[plane],
                 dst_ref=vhalo.at[way],
@@ -233,7 +236,7 @@
                 recv_sem=h_recv.at[2 * way + 1],
                 device_id=device,
                 device_id_type=MESH,
-            )
+            ),
         )
 
     def send_half(half):
@@ -250,8 +253,13 @@
     send_half(0)
     cut(1)
     send_half(1)
-    for copy in halos:
-        copy.start()
+    for way in range(2):
+
+        @pl.when(sides[way][0])
+        def _():
+            for copy in halo_copies(way):
+                copy.start()
+
     x_all[c * CHIPS + h] = x_msg[...]
     pall[c * CHIPS + h] = ploc[h]
 
@@ -392,19 +400,32 @@
     for line in range(NY):
         share(c, line).wait_send()
 
-    for copy in halos:
-        copy.wait()
-    low = jnp.where(gx == 0, 0.0, 1.0).astype(F32)
-    high = jnp.where(gx == NZ - 1, 0.0, 1.0).astype(F32)
+    for way in range(2):
+
+        @pl.when(sides[way][0])
+        def _():
+            for copy in halo_copies(way):
+                copy.wait_send()
+
+        @pl.when(sides[1 - way][0])
+        def _():
+            for copy in halo_copies(way):
+                copy.wait_recv()
+
+        @pl.when(jnp.logical_not(sides[1 - way][0]))
+        def _():
+            mhalo[way] = jnp.zeros(mhalo.shape[1:], F32)
+            vhalo[way] = jnp.zeros(vhalo.shape[1:], F32)
+
 
     def advect(t, _):
         rows = pl.ds(pl.multiple_of(t * 8, 8), 8)
-        vel = [vhalo[0, rows, :] * low] + [velocity[i, rows, :] for i in range(8)]
-        vel = vel + [vhalo[1, rows, :] * high]
+        vel = [vhalo[0, rows, :]] + [velocity[i, rows, :] for i in range(8)]
+        vel = vel + [vhalo[1, rows, :]]
         face = [0.5 * (vel[i] + vel[i + 1]) for i in range(9)]
         for m in range(4):
-            mark = [mhalo[0, m, rows, :] * low] + [markers[m, i, rows, :] for i in range(8)]
-            mark = mark + [mhalo[1, m, rows, :] * high]
+            mark = [mhalo[0, m, rows, :]] + [markers[m, i, rows, :] for i in range(8)]
+            mark = mark + [mhalo[1, m, rows, :]]
             flux = [face[i] * jnp.where(face[i] > 0, mark[i], mark[i + 1]) for i in range(9)]
             for i in range(8):
                 here = mark[i + 1]

time: 50.5 us -> 44.3 us (0.88)
  Pallas kernels: 49.7 us -> 43.5 us
    pallas_call x1, Pallas kernels: 48.3 us -> 42.1 us  [exchange(): pl.pallas_call(exchange_kernel, out_shape=(pltpu.VMEM(markers.shape, F32)...]
where the time goes in v4:
time: 44.3 us; the launch traced here: 44.1 us
  Pallas kernels  43.5 us (98%)
  between operations  0.64 us (1%)
    pallas_call x1, Pallas kernels, exchange(): pl.pallas_call(exchange_kernel, out_shape=(pltpu.VMEM(markers.shape, F32)...  42.1 us
    pallas_call x1, Pallas kernels, write(): pl.pallas_call(write_kernel, out_shape=(jax.ShapeDtypeStruct(adv.shape, F...  1.38 us

profile of v4, /device:TPU:1, one launch (start us, length us, event | category | flops | bytes accessed | tf_op | source)
XLA Modules:
  0.0 44.1 jit_solution(6393825245095883049)
XLA Ops:
  0.6 42.1 %shard_map.77 = (f32[4,8,64,128]{3,2,1,0:T(8,128)S(1)}, f32[64,4096]{1,0:T(8,128)S(1)}) custom-call(s32[4,64]{1,0:T(4,128)} %boxes_hbm.1, s32[2,64]{1,0:T(2,128)} %bitcast.7, s32[2,64]{1,0:T(2,128)} %bitcast.8, s32[1,64]{1,0:T(1,128)} %bitcast.9, f32[4,8,64,128]{3,2,1,0:T(8,128)} %markers_hbm.1, f32[8,64,128]{2,1,0:T(8,128)} %velocity_hbm.1), custom_call_target="tpu_custom_call" | custom-call | tf_op jit(solution)/shard_map/pallas_call | solution.py:467
  42.8 1.4 %shard_map.78 = (f32[4,8,64,128]{3,2,1,0:T(8,128)}, f32[64,4096]{1,0:T(8,128)}) custom-call(f32[4,8,64,128]{3,2,1,0:T(8,128)S(1)} %get-tuple-element.4.adv, f32[64,4096]{1,0:T(8,128)S(1)} %get-tuple-element.5.force), custom_call_target="tpu_custom_call" | custom-call | tf_op jit(solution)/shard_map/pallas_call | solution.py:527

commit v5 on v4

--- a/solution.py
+++ b/solution.py
@@ -87,18 +87,6 @@
     sibling = (gx, gy, y * 2 + other)
     sides = ((gx < NZ - 1, (gx + 1, gy, gz), 7), (gx > 0, (gx - 1, gy, gz), 0))
 
-    loads = []
-    for src, dst in (
-        (boxes_hbm, boxes),
-        (send_hbm, send_pick),
-        (recv_hbm, recv_pick),
-        (count_hbm, count),
-        *((markers_hbm.at[m], markers.at[m]) for m in range(4)),
-        (velocity_hbm, velocity),
-    ):
-        loads.append(pltpu.make_async_copy(src, dst, in_sem.at[len(loads)]))
-        loads[-1].start()
-
     ys = [lax.rem(y + dy, NY) for dy in range(NY)]
     xs = [lax.rem(gy + dx, NX) for dx in range(NX)]
     base = [[lax.rem(parity + i, 2) * HALF + xs[dx] // 2 for dx in range(NX)] for i in range(2)]
@@ -140,14 +128,18 @@
         def _():
             pl.semaphore_signal(barrier, inc=1, device_id=device, device_id_type=MESH)
 
-
-    for copy in loads:
-        copy.wait()
-
-    for s in range(2):
-        far = jnp.where(count[...] > s, send_pick[s : s + 1, :].astype(F32), UNUSED)
-        x_msg[s : s + 1, 0:BUB] = far
-        x_msg[s : s + 1, BUB:LANES] = recv_pick[s : s + 1, :].astype(F32)
+    loads = []
+    for src, dst in (
+        (boxes_hbm, boxes),
+        *((markers_hbm.at[m], markers.at[m]) for m in range(4)),
+        (send_hbm, send_pick),
+        (recv_hbm, recv_pick),
+        (count_hbm, count),
+        (velocity_hbm, velocity),
+    ):
+        loads.append(pltpu.make_async_copy(src, dst, in_sem.at[len(loads)]))
+    for copy in loads[:-1]:
+        copy.start()
 
     group = iota((8, LANES), 1) // PATCH
     rows = markers.reshape(4 * 8 * 64, LANES)
@@ -160,20 +152,30 @@
                 cells = None
                 for j in range(4):
                     piece = rows[pl.ds(base + (2 * half + dx) * 64 + j, 8, stride=4), :]
-                    piece = pltpu.roll(piece, lax.rem(PATCH * j - z0 + LANES, LANES), 1)
+                    piece = pltpu.roll(piece, jnp.bitwise_and(PATCH * j - z0 + LANES, LANES - 1), 1)
                     cells = piece if j == 0 else jnp.where(group == j, piece, cells)
                 tmp[pl.ds(pl.multiple_of(b * HALF + dx * 8, 8), 8), :] = cells
             return 0
 
-        lax.fori_loop(0, BUB, one, 0, unroll=8)
+        lax.fori_loop(0, BUB, one, 0, unroll=16)
 
         def put(s, _):
             ploc[half * HALF + s] = tmp[pl.ds(s, BUB, stride=HALF), :].astype(BF16)
             return 0
 
-        lax.fori_loop(0, HALF, put, 0, unroll=4)
-
+        lax.fori_loop(0, HALF, put, 0, unroll=8)
+
+    for copy in loads[:5]:
+        copy.wait()
     cut(0)
+    loads[-1].start()
+    for copy in loads[5:-1]:
+        copy.wait()
+
+    for s in range(2):
+        far = jnp.where(count[...] > s, send_pick[s : s + 1, :].astype(F32), UNUSED)
+        x_msg[s : s + 1, 0:BUB] = far
+        x_msg[s : s + 1, BUB:LANES] = recv_pick[s : s + 1, :].astype(F32)
 
     neighbours = jnp.where(gx < NZ - 1, 1, 0) + jnp.where(gx > 0, 1, 0)
     pl.semaphore_wait(barrier, CHIPS + neighbours)
@@ -239,20 +241,21 @@
             ),
         )
 
-    def send_half(half):
+    def send_half(copy, half):
         found = others_in(half)
         for to, device in found[:-1]:
-            p_copy(to, device).start()
+            copy(to, device).start()
 
         @pl.when(parity != half)
         def _():
-            p_copy(*found[-1]).start()
-
-    for to, device in others:
-        x_copy(to, device).start()
-    send_half(0)
+            copy(*found[-1]).start()
+
+    send_half(x_copy, 0)
+    send_half(p_copy, 0)
+    send_half(x_copy, 1)
     cut(1)
-    send_half(1)
+    send_half(p_copy, 1)
+    loads[-1].wait()
     for way in range(2):
 
         @pl.when(sides[way][0])
@@ -262,6 +265,32 @@
 
     x_all[c * CHIPS + h] = x_msg[...]
     pall[c * CHIPS + h] = ploc[h]
+
+    row = iota((256, LANES), 0)
+    lane = iota((256, LANES), 1)
+    from_peer = peer_at(row // 8, c)
+    slot = lax.rem(row, 4)
+    spread = []
+    for s in range(2):
+        hit = (lax.rem(slot, 2) == s) & (lane == from_peer + jnp.where(slot < 2, 0, BUB))
+        spread.append(jnp.where(hit, 1.0, 0.0).astype(BF16))
+    wanted = (lane - BUB * lax.rem(row // 4, 2)).astype(F32)
+
+    row = iota((LANES, 256), 0)
+    lane = iota((LANES, 256), 1)
+    to_peer = peer_at(lax.rem(lane // 4, CHIPS), lane // LANES)
+    slot = lax.rem(lane, 4)
+    order = []
+    for s in range(2):
+        hit = (lax.rem(slot, 2) == s) & (row == to_peer + jnp.where(slot < 2, BUB, 0))
+        order.append(jnp.where(hit, 1.0, 0.0).astype(BF16))
+
+    half_row = iota((256, CHIPS), 0)
+    half_lane = iota((256, CHIPS), 1)
+    pair_half = lax.rem(half_lane, 2) == lax.rem(half_row // 4, 2)
+    pair_of = iota((CHIPS, LANES), 0) // 2
+
+    bubble = iota((BUB, 2 * LANES), 0).astype(F32)
 
     for frm, _ in others:
         landed(x_all, c * CHIPS + frm, x_send, x_recv, frm).wait_recv()
@@ -275,30 +304,6 @@
     )
     x_share.start()
 
-    row = iota((256, LANES), 0)
-    lane = iota((256, LANES), 1)
-    from_peer = peer_at(row // 8, c)
-    slot = lax.rem(row, 4)
-    spread = []
-    for s in range(2):
-        hit = (lax.rem(slot, 2) == s) & (lane == from_peer + jnp.where(slot < 2, 0, BUB))
-        spread.append(jnp.where(hit, 1.0, 0.0).astype(BF16))
-    wanted = (lane - BUB * lax.rem(row // 4, 2)).astype(F32)
-
-    row = iota((LANES, 256), 0)
-    lane = iota((LANES, 256), 1)
-    to_peer = peer_at(lax.rem(lane // 4, CHIPS), lane // LANES)
-    slot = lax.rem(lane, 4)
-    order = []
-    for s in range(2):
-        hit = (lax.rem(slot, 2) == s) & (row == to_peer + jnp.where(slot < 2, BUB, 0))
-        order.append(jnp.where(hit, 1.0, 0.0).astype(BF16))
-
-    half_row = iota((256, CHIPS), 0)
-    half_lane = iota((256, CHIPS), 1)
-    pair_half = lax.rem(half_lane, 2) == lax.rem(half_row // 4, 2)
-    pair_of = iota((CHIPS, LANES), 0) // 2
-
     def gather_matrices(core):
         wide = jnp.zeros((256, CHIPS), F32)
         for s in range(2):
@@ -328,7 +333,6 @@
             preferred_element_type=F32,
         )
     nidx[...] = index
-    bubble = iota((BUB, 2 * LANES), 0).astype(F32)
 
     def sum_matrix(q, _):
         nbuf[q] = jnp.where(bubble == nidx[pl.ds(q, 1), :], 1.0, 0.0).astype(BF16)

time: 44.3 us -> 44.5 us (level)
  no operation moved by 1% of the time
where the time goes in v5:
time: 44.5 us; the launch traced here: 44.3 us
  Pallas kernels  43.7 us (98%)
  between operations  0.64 us (1%)
    pallas_call x1, Pallas kernels, exchange(): pl.pallas_call(exchange_kernel, out_shape=(pltpu.VMEM(markers.shape, F32)...  42.3 us
    pallas_call x1, Pallas kernels, write(): pl.pallas_call(write_kernel, out_shape=(jax.ShapeDtypeStruct(adv.shape, F...  1.38 us

profile of v5, /device:TPU:1, one launch (start us, length us, event | category | flops | bytes accessed | tf_op | source)
XLA Modules:
  0.0 44.3 jit_solution(3001609192295969007)
XLA Ops:
  0.6 42.3 %shard_map.77 = (f32[4,8,64,128]{3,2,1,0:T(8,128)S(1)}, f32[64,4096]{1,0:T(8,128)S(1)}) custom-call(s32[4,64]{1,0:T(4,128)} %boxes_hbm.1, s32[2,64]{1,0:T(2,128)} %bitcast.7, s32[2,64]{1,0:T(2,128)} %bitcast.8, s32[1,64]{1,0:T(1,128)} %bitcast.9, f32[4,8,64,128]{3,2,1,0:T(8,128)} %markers_hbm.1, f32[8,64,128]{2,1,0:T(8,128)} %velocity_hbm.1), custom_call_target="tpu_custom_call" | custom-call | tf_op jit(solution)/shard_map/pallas_call | solution.py:471
  42.9 1.4 %shard_map.78 = (f32[4,8,64,128]{3,2,1,0:T(8,128)}, f32[64,4096]{1,0:T(8,128)}) custom-call(f32[4,8,64,128]{3,2,1,0:T(8,128)S(1)} %get-tuple-element.4.adv, f32[64,4096]{1,0:T(8,128)S(1)} %get-tuple-element.5.force), custom_call_target="tpu_custom_call" | custom-call | tf_op jit(solution)/shard_map/pallas_call | solution.py:531

commit v6 on v5

--- a/solution.py
+++ b/solution.py
@@ -371,6 +371,8 @@
                     landed(pall, c * CHIPS + frm, p_send, p_recv, frm).wait_recv()
 
             share(c, line).start()
+
+    for half in range(2):
         gather(c, half)
 
     x_share.wait()

time: 44.5 us -> 44.4 us (level)
  no operation moved by 1% of the time
where the time goes in v6:
time: 44.4 us; the launch traced here: 44.2 us
  Pallas kernels  43.6 us (98%)
  between operations  0.64 us (1%)
    pallas_call x1, Pallas kernels, exchange(): pl.pallas_call(exchange_kernel, out_shape=(pltpu.VMEM(markers.shape, F32)...  42.2 us
    pallas_call x1, Pallas kernels, write(): pl.pallas_call(write_kernel, out_shape=(jax.ShapeDtypeStruct(adv.shape, F...  1.38 us

profile of v6, /device:TPU:1, one launch (start us, length us, event | category | flops | bytes accessed | tf_op | source)
XLA Modules:
  0.0 44.2 jit_solution(7577437062523171002)
XLA Ops:
  0.6 42.2 %shard_map.77 = (f32[4,8,64,128]{3,2,1,0:T(8,128)S(1)}, f32[64,4096]{1,0:T(8,128)S(1)}) custom-call(s32[4,64]{1,0:T(4,128)} %boxes_hbm.1, s32[2,64]{1,0:T(2,128)} %bitcast.7, s32[2,64]{1,0:T(2,128)} %bitcast.8, s32[1,64]{1,0:T(1,128)} %bitcast.9, f32[4,8,64,128]{3,2,1,0:T(8,128)} %markers_hbm.1, f32[8,64,128]{2,1,0:T(8,128)} %velocity_hbm.1), custom_call_target="tpu_custom_call" | custom-call | tf_op jit(solution)/shard_map/pallas_call | solution.py:473
  42.8 1.4 %shard_map.78 = (f32[4,8,64,128]{3,2,1,0:T(8,128)}, f32[64,4096]{1,0:T(8,128)}) custom-call(f32[4,8,64,128]{3,2,1,0:T(8,128)S(1)} %get-tuple-element.4.adv, f32[64,4096]{1,0:T(8,128)S(1)} %get-tuple-element.5.force), custom_call_target="tpu_custom_call" | custom-call | tf_op jit(solution)/shard_map/pallas_call | solution.py:533
